TPU v7x, 256 devices: a whole 4x4x8 slice. The times are simulated.
256 devices in a mesh: role: 2 (over core), req: 16 (over x, y), tp: 8 (over z).
Axes of the slice: x: 4, y: 4, z: 8, core: 2. Of those that a mesh axis runs over, the one named last changes fastest.
Arguments:
- decode_hidden: bfloat16 [2, 128, 8192], P('role', None, 'req'), may hold values from -400 to 400
- span_hidden: bfloat16 [2, 1024, 8192], P('role', 'req'), may hold values from -400 to 400
- norm_gain: bfloat16 [8192], replicated, may hold values from 0.25 to 1.75
- w_query: bfloat16 [8192, 8192], P('req', 'tp'), may hold values from -0.0625 to 0.0625
- w_keyval: bfloat16 [8192, 2048], P(None, 'tp'), may hold values from -0.0625 to 0.0625
- w_out: bfloat16 [8192, 8192], P('tp', 'req'), may hold values from -0.0625 to 0.0625
- cache: bfloat16 [2, 128, 1024, 2048], P('role', 'req', None, 'tp'), may hold values from -400 to 400
- lengths: int32 [2, 128], P('role', 'req'), may hold values from 128 to 1024, as said below
- route: int32 [2, 1024, 3], P('role', 'req'), may hold values from 0 to 127, as said below
Outputs:
- decoded: bfloat16 [2, 128, 8192], P('role', None, 'req')
Inputs may be any that keep to these rules, and one draw needn't show every extreme that they name: `route`: each row is (owner, request, slot): owner < 32 names pool owner // 16, request < 8 counts among that owner's requests, slot < 128. No two rows share owner, request and slot. Of the 64 rows of one device, at most 4 go to one owner, and one owner receives exactly 4 from every device. `lengths`: some request has exactly 1024.
All inputs are finite; a program needn't handle non-finite values.
Results may differ from a plain program's by a relative error of at most 0.034.
Values may be sent and summed in bfloat16 or wider, within the bound.
A program may use at most 128 MiB of HBM per device.

v0:
```python
import jax
import jax.numpy as jnp
from jax import lax
from jax.sharding import PartitionSpec as P

D = 8192
QH = 64
KVH = 8
HD = 128
STEPS = 2


EPS = 1e-05
BASE = 500000.0
FLOOR = -1e30


def rotate(vec, pos):
    half = vec.shape[-1] // 2
    freq = BASE ** (-jnp.arange(half, dtype=jnp.float32) / half)
    angle = pos[..., None].astype(jnp.float32) * freq
    cosine = jnp.cos(angle)
    sine = jnp.sin(angle)
    first = vec[..., :half]
    second = vec[..., half:]
    return jnp.concatenate(
        [first * cosine - second * sine, second * cosine + first * sine], axis=-1
    )


def scaled_rows(rows, gain):
    wide = rows.astype(jnp.float32)
    scale = lax.rsqrt(jnp.mean(wide * wide, axis=-1) + EPS)
    mixed = (wide * gain.astype(jnp.float32)).astype(jnp.bfloat16)
    return (mixed, scale)


def attend_block(query, cache_rows, lengths, fresh_keys, fresh_values):
    count, ctx_len, _ = cache_rows.shape
    kv_local = query.shape[1]
    blocks = cache_rows.reshape(count, ctx_len, kv_local, 2, HD)
    keys = blocks[:, :, :, 0]
    values = blocks[:, :, :, 1]
    inverse = HD ** (-0.5)
    old = jnp.einsum("rgjd,rcgd->rgjc", query, keys, preferred_element_type=jnp.float32) * inverse
    new = (
        jnp.einsum("rgjd,rngd->rgjn", query, fresh_keys, preferred_element_type=jnp.float32)
        * inverse
    )
    live = (jnp.arange(ctx_len)[None, :] < lengths[:, None])[:, None, None, :]
    top = jnp.maximum(jnp.max(jnp.where(live, old, FLOOR), axis=-1), jnp.max(new, axis=-1))
    old_exp = jnp.where(live, jnp.exp(old - top[..., None]), 0.0)
    new_exp = jnp.exp(new - top[..., None])
    total = jnp.sum(old_exp, axis=-1) + jnp.sum(new_exp, axis=-1)
    weight_old = (old_exp / total[..., None]).astype(jnp.bfloat16)
    weight_new = (new_exp / total[..., None]).astype(jnp.bfloat16)
    out = jnp.einsum("rgjc,rcgd->rgjd", weight_old, values, preferred_element_type=jnp.float32)
    out = out + jnp.einsum(
        "rgjn,rngd->rgjd", weight_new, fresh_values, preferred_element_type=jnp.float32
    )
    return out.astype(jnp.bfloat16).reshape(count, -1)


def decode_step(
    hidden,
    gain_slice,
    w_query,
    key_slice,
    w_out,
    cache_own,
    lengths,
    step,
    fresh_keys,
    fresh_values,
):
    rows = hidden.astype(jnp.float32)
    local_squares = jnp.sum(rows * rows, axis=1)
    mixed = (rows * gain_slice.astype(jnp.float32)).astype(jnp.bfloat16)
    local = lengths.shape[0]
    pieces = [
        jnp.dot(mixed, w_query, preferred_element_type=jnp.float32),
        jnp.dot(mixed, key_slice, preferred_element_type=jnp.float32),
    ]
    projected = lax.psum_scatter(
        jnp.concatenate(pieces, axis=1), "req", scatter_dimension=0, tiled=True
    )
    squares = lax.psum(local_squares, "req")
    scale = lax.rsqrt(squares / D + EPS)
    own_scale = lax.dynamic_slice_in_dim(scale, lax.axis_index("req") * local, local, 0)
    projected = projected * own_scale[:, None]
    kv_local = key_slice.shape[1] // (2 * HD)
    group = QH // KVH
    query_cols = kv_local * group * HD
    position = (lengths + step)[:, None]
    query = rotate(projected[:, :query_cols].reshape(local, kv_local * group, HD), position)
    query = query.astype(jnp.bfloat16).reshape(local, kv_local, group, HD)
    keyval = projected[:, query_cols:].reshape(local, kv_local, 2, HD)
    fresh_keys = fresh_keys + [rotate(keyval[:, :, 0], position).astype(jnp.bfloat16)]
    fresh_values = fresh_values + [keyval[:, :, 1].astype(jnp.bfloat16)]
    heads = attend_block(
        query, cache_own, lengths, jnp.stack(fresh_keys, axis=1), jnp.stack(fresh_values, axis=1)
    )
    partial_value = jnp.dot(
        lax.all_gather(heads, "req", axis=0, tiled=True), w_out, preferred_element_type=jnp.float32
    )
    total = lax.psum(partial_value, "tp")
    result = (rows + total).astype(jnp.bfloat16)
    return (result, fresh_keys, fresh_values)


def on_device(
    decode_hidden, span_hidden, norm_gain, w_query, w_keyval, w_out, cache, lengths, route
):
    req_count = lax.axis_size("req")
    owner_index = lax.axis_index("req")
    width = decode_hidden.shape[2]
    gain_slice = lax.dynamic_slice_in_dim(norm_gain, owner_index * width, width, 0)
    key_slice = lax.dynamic_slice_in_dim(w_keyval, owner_index * width, width, 0)
    mixed, scale = scaled_rows(span_hidden[0], norm_gain)
    count = mixed.shape[0]
    keyval = (
        jnp.dot(mixed, w_keyval, preferred_element_type=jnp.float32) * scale[:, None]
    ).reshape(count, -1, 2, HD)
    plan = route[0]
    slot = plan[:, 2]
    rotated = rotate(keyval[:, :, 0], slot[:, None])
    packed = jnp.stack([rotated, keyval[:, :, 1]], axis=2).reshape(count, -1).astype(jnp.bfloat16)
    owners = 2 * req_count
    limit = count // req_count
    onehot = (plan[:, 0:1] == jnp.arange(owners)[None, :]).astype(jnp.int32)
    rank = jnp.sum(jnp.cumsum(onehot, axis=0) * onehot, axis=1) - 1
    place = plan[:, 0] * limit + rank
    tags = jnp.stack([plan[:, 1] + 1, slot // 64, slot % 64], axis=1).astype(jnp.bfloat16)
    outbox = jnp.zeros((owners * limit, packed.shape[1]), jnp.bfloat16).at[place].set(packed)
    labels = jnp.zeros((owners * limit, 3), jnp.bfloat16).at[place].set(tags)
    inbox, marks = (
        lax.all_to_all(
            outbox.reshape(owners, limit, -1),
            ("role", "req"),
            split_axis=0,
            concat_axis=0,
            tiled=True,
        ),
        lax.all_to_all(
            labels.reshape(owners, limit, 3),
            ("role", "req"),
            split_axis=0,
            concat_axis=0,
            tiled=True,
        ),
    )
    inbox = inbox.reshape(owners * limit, -1)
    marks = marks.reshape(owners * limit, 3).astype(jnp.int32)
    ctx_len = cache.shape[2]
    filled = marks[:, 0] > 0
    target = jnp.where(filled, marks[:, 1] * 64 + marks[:, 2], ctx_len)
    request = jnp.where(filled, marks[:, 0] - 1, 0)
    cache_own = cache[0].at[request, target].set(inbox, mode="drop")
    hidden = decode_hidden[0]
    fresh_keys = []
    fresh_values = []
    for step in range(STEPS):
        hidden, fresh_keys, fresh_values = decode_step(
            hidden,
            gain_slice,
            w_query,
            key_slice,
            w_out,
            cache_own,
            lengths[0],
            step,
            fresh_keys,
            fresh_values,
        )
    return hidden[None]


def solution(mesh):
    placed = (
        P("role", None, "req"),
        P("role", "req", None),
        P(),
        P("req", "tp"),
        P(None, "tp"),
        P("tp", "req"),
        P("role", "req", None, "tp"),
        P("role", "req"),
        P("role", "req", None),
    )
    return jax.shard_map(
        on_device, mesh=mesh, in_specs=placed, out_specs=P("role", None, "req"), check_vma=False
    )
```

profile of v0, /device:TPU:24, one launch (start us, length us, event | category | flops | bytes accessed | tf_op | source)
XLA Modules:
  0.0 430.9 jit_solution(5316805459011930639)
XLA Ops:
  6.5 4.5 %copy.153 = bf16[1,8,1024,256]{3,2,1,0:T(8,128)(2,1)} copy(bf16[1,8,1024,256]{3,2,1,0:T(8,128)(2,1)} %param.15) | data formatting | bytes 8388608
  11.6 0.8 scatter_custom_fusion
  12.4 0.9 copy.99
  13.3 7.3 %all-to-all-start = ((bf16[32,4,3]{1,2,0:T(4,128)(2,1)}), bf16[32,4,3]{1,2,0:T(4,128)(2,1)S(1)}, u32[]{:S(2)}, u32[]{:S(2)}) async-start(bf16[32,4,3]{1,2,0:T(4,128)(2,1)} %copy.99), calls=%async_computation | async-start | bytes 65536 | tf_op jit(solution)/shard_map/all_to_all | solution.py:144
  20.7 1.1 fusion.25
  22.2 0.9 pad_maximum_fusion
  23.5 3.0 convolution_multiply_fusion
  27.1 0.8 scatter_custom_fusion.1
  28.7 32.5 %psum.28 = f32[128]{0:T(128)S(1)} all-reduce(f32[128]{0:T(128)S(1)} %fusion.21), channel_id=1, replica_groups=mesh['role'=2,'req'=16,'tp'=8] {'req'}, use_global_device_ids=true, to_apply=%region_2.3 | all-reduce | flops 128 | bytes 1024 | tf_op jit(solution)/shard_map/psum | solution.py:87
  62.7 11.8 %all-to-all-start.1 = ((bf16[32,4,256]{2,1,0:T(4,128)(2,1)}), bf16[32,4,256]{2,1,0:T(4,128)(2,1)S(1)}, u32[]{:S(2)}, u32[]{:S(2)}) async-start(bf16[32,4,256]{2,1,0:T(4,128)(2,1)} %reshape.666), calls=%async_computation.1 | async-start | bytes 131072 | tf_op jit(solution)/shard_map/all_to_all | solution.py:137
  75.0 5.4 %all-to-all-done.1 = bf16[32,4,256]{2,1,0:T(4,128)(2,1)S(1)} async-done(((bf16[32,4,256]{2,1,0:T(4,128)(2,1)}), bf16[32,4,256]{2,1,0:T(4,128)(2,1)S(1)}, u32[]{:S(2)}, u32[]{:S(2)}) %all-to-all-start.1) | async-done | bytes 65568 | tf_op jit(solution)/shard_map/all_to_all | solution.py:137
  80.4 16.1 %scatter_fusion = bf16[8,1024,256]{2,1,0:T(8,128)(2,1)} fusion(bf16[8,1024,256]{2,1,0:T(8,128)(2,1)} %bitcast.140, s32[128]{0:T(128)S(1)} %fusion.97, bf16[128,256]{1,0:T(8,128)(2,1)S(1)} %reshape.701), kind=kCustom, calls=%fused_computation.2 | custom fusion | bytes 197632 | tf_op jit(solution)/shard_map/scatter | solution.py:158
  96.5 6.4 %copy.105 = bf16[8,1024,256]{1,2,0:T(8,128)(2,1)} copy(bf16[8,1024,256]{2,1,0:T(8,128)(2,1)} %scatter_fusion) | data formatting | bytes 8388608 | tf_op jit(solution)/shard_map/scatter | solution.py:158
  102.9 19.4 %all-reduce.11.cloned.1.call-done = f32[128,1280]{1,0:T(8,128)} async-done(((f32[128,1280]{1,0:T(8,128)}), f32[128,1280]{1,0:T(8,128)}) %all-reduce.11.cloned.1.call-update) | async-done | bytes 655376
  122.3 0.8 dynamic-slice_multiply_fusion.1
  123.7 2.1 select_reduce_fusion.1
  126.1 2.3 fusion.12
  128.4 21.7 %all_gather.6 = bf16[128,1024]{1,0:T(8,128)(2,1)S(1)} all-gather(bf16[8,1024]{1,0:T(8,128)(2,1)S(1)} %bitcast.150), channel_id=1, replica_groups=mesh['role'=2,'req'=16,'tp'=8] {'req'}, dimensions={0}, use_global_device_ids=true | all-gather | bytes 278528 | tf_op jit(solution)/shard_map/all_gather | solution.py:104
  150.1 1.0 fusion.109
  151.2 72.8 %all-reduce.7.cloned.1.call-done = f32[128,512]{1,0:T(8,128)} async-done(((f32[128,512]{1,0:T(8,128)}), f32[128,512]{1,0:T(8,128)}) %all-reduce.7.cloned.1.call-update) | async-done | bytes 262160 | tf_op jit(solution)/shard_map/psum | solution.py:106
  224.0 1.1 fusion.18
  225.1 1.1 fusion.23
  226.5 0.9 pad_maximum_fusion.1
  227.5 32.5 %psum.30 = f32[128]{0:T(128)S(1)} all-reduce(f32[128]{0:T(128)S(1)} %get-tuple-element.5), channel_id=1, replica_groups=mesh['role'=2,'req'=16,'tp'=8] {'req'}, use_global_device_ids=true, to_apply=%region_14.15 | all-reduce | flops 128 | bytes 1024 | tf_op jit(solution)/shard_map/psum | solution.py:87
  260.1 60.8 %all-reduce.13.cloned.1.call-done = f32[128,1280]{1,0:T(8,128)} async-done(((f32[128,1280]{1,0:T(8,128)}), f32[128,1280]{1,0:T(8,128)}) %all-reduce.13.cloned.1.call-update) | async-done | bytes 655376
  320.9 0.8 dynamic-slice_multiply_fusion
  322.0 2.1 select_reduce_fusion
  324.8 2.3 fusion.13
  327.1 21.7 %all_gather.7 = bf16[128,1024]{1,0:T(8,128)(2,1)S(1)} all-gather(bf16[8,1024]{1,0:T(8,128)(2,1)S(1)} %bitcast.151), channel_id=1, replica_groups=mesh['role'=2,'req'=16,'tp'=8] {'req'}, dimensions={0}, use_global_device_ids=true | all-gather | bytes 278528 | tf_op jit(solution)/shard_map/all_gather | solution.py:104
  348.8 1.0 fusion.110
  349.8 72.9 %all-reduce.9.cloned.1.call-done = f32[128,512]{1,0:T(8,128)} async-done(((f32[128,512]{1,0:T(8,128)}), f32[128,512]{1,0:T(8,128)}) %all-reduce.9.cloned.1.call-update) | async-done | bytes 262160 | tf_op jit(solution)/shard_map/psum | solution.py:106
  422.7 1.6 fusion.29
  (99 shorter events, 5.9 us)
Async XLA Ops:
  6.5 15.3 %copy-start = (bf16[512,1024]{1,0:T(8,128)(2,1)S(1)}, bf16[512,1024]{1,0:T(8,128)(2,1)}, u32[]{:S(2)}) copy-start(bf16[512,1024]{1,0:T(8,128)(2,1)} %param.12) | copy-start | bytes 3145732
  6.5 14.2 %copy-start.3 = (bf16[1,128,512]{2,1,0:T(8,128)(2,1)S(1)}, bf16[1,128,512]{2,1,0:T(8,128)(2,1)}, u32[]{:S(2)}) copy-start(bf16[1,128,512]{2,1,0:T(8,128)(2,1)} %param.9) | copy-start | bytes 393220
  6.5 14.1 %copy-start.4 = (bf16[8192]{0:T(1024)(128)(2,1)S(1)}, bf16[8192]{0:T(1024)(128)(2,1)}, u32[]{:S(2)}) copy-start(bf16[8192]{0:T(1024)(128)(2,1)} %param.11) | copy-start | bytes 49156
  6.5 4.5 %copy-start.5 = (s32[1,64,3]{1,0,2:T(1,128)S(1)}, s32[1,64,3]{1,0,2:T(1,128)}, u32[]{:S(2)}) copy-start(s32[1,64,3]{1,0,2:T(1,128)} %param.17) | copy-start | bytes 2308
  11.1 12.1 %copy-start.2 = (bf16[1,64,8192]{2,1,0:T(8,128)(2,1)S(1)}, bf16[1,64,8192]{2,1,0:T(8,128)(2,1)}, u32[]{:S(2)}) copy-start(bf16[1,64,8192]{2,1,0:T(8,128)(2,1)} %param.10) | copy-start | bytes 3145732
  13.3 49.5 %all-to-all-start = ((bf16[32,4,3]{1,2,0:T(4,128)(2,1)}), bf16[32,4,3]{1,2,0:T(4,128)(2,1)S(1)}, u32[]{:S(2)}, u32[]{:S(2)}) async-start(bf16[32,4,3]{1,2,0:T(4,128)(2,1)} %copy.99), calls=%async_computation | async-start | bytes 65536 | tf_op jit(solution)/shard_map/all_to_all | solution.py:144
  20.6 101.8 %all-reduce.11.cloned.1.call-start = ((), (), s32[]{:S(2)}) async-start(), calls=%async_computation.4 | async-start | bytes 1310720
  22.2 4.5 %copy-start.6 = (s32[1,8]{1,0:T(1,128)S(1)}, s32[1,8]{1,0:T(1,128)}, u32[]{:S(2)}) copy-start(s32[1,8]{1,0:T(1,128)} %param.16) | copy-start | bytes 100
  23.1 38.3 %copy-start.7 = (u32[256]{0:T(256)S(1)}, u32[256]{0:T(256)}, u32[]{:S(2)}) copy-start(u32[256]{0:T(256)} %constant.112) | copy-start | bytes 3076
  62.7 17.7 %all-to-all-start.1 = ((bf16[32,4,256]{2,1,0:T(4,128)(2,1)}), bf16[32,4,256]{2,1,0:T(4,128)(2,1)S(1)}, u32[]{:S(2)}, u32[]{:S(2)}) async-start(bf16[32,4,256]{2,1,0:T(4,128)(2,1)} %reshape.666), calls=%async_computation.1 | async-start | bytes 131072 | tf_op jit(solution)/shard_map/all_to_all | solution.py:137
  74.6 149.4 %all-reduce.7.cloned.1.call-start = ((), (), s32[]{:S(2)}) async-start(), calls=%async_computation.2 | async-start | bytes 524288 | tf_op jit(solution)/shard_map/psum | solution.py:106
  102.9 47.1 %copy-start.1 = (bf16[1024,512]{1,0:T(8,128)(2,1)S(1)}, bf16[1024,512]{1,0:T(8,128)(2,1)}, u32[]{:S(2)}) copy-start(bf16[1024,512]{1,0:T(8,128)(2,1)} %param.14) | copy-start | bytes 3145732
  151.1 169.8 %all-reduce.13.cloned.1.call-start = ((), (), s32[]{:S(2)}) async-start(), calls=%async_computation.5 | async-start | bytes 1310720
  227.5 195.3 %all-reduce.9.cloned.1.call-start = ((), (), s32[]{:S(2)}) async-start(), calls=%async_computation.3 | async-start | bytes 524288 | tf_op jit(solution)/shard_map/psum | solution.py:106
Sparse Core Ops, SparseCore 0:
  24.7 97.6 all-reduce.10
  151.2 72.7 all-reduce.6
  227.6 93.2 all-reduce.12
  350.0 72.7 all-reduce.8
where the time goes:
time: 432 us; the launch traced here: 431 us
  waiting for transfers between devices  231 us (53%)
  blocking collectives  108 us (25%)
  local copies, waits for them, and re-layouts  31.7 us (7%)
  starting transfers between devices  19.3 us (4%)
  matrix products  17.3 us (4%)
  between operations  14.2 us (3%)
  other arithmetic  8.59 us (2%)
    psum x2, waiting for transfers between devices, decode_step(): total = lax.psum(partial_value, 'tp')  146 us
    unnamed x6, waiting for transfers between devices  80.3 us
    psum x2, blocking collectives, decode_step(): squares = lax.psum(local_squares, 'req')  65 us
    all_gather x2, blocking collectives, decode_step(): lax.all_gather(heads, 'req', axis=0, tiled=True)  43.4 us
    scatter x2, local copies, waits for them, and re-layouts, on_device(): cache_own = cache[0].at[request, target].set(inbox, mode='drop')  22.5 us
    all_to_all x1, starting transfers between devices, on_device(): lax.all_to_all(outbox.reshape(owners, limit, -1), ('role', 'req'), split_...  11.8 us
  transfers between devices with their start and end apart: 6, of which 5 were waited for; matrix products, arithmetic and copies ran while one was open for 7% of the time, Pallas kernels for 0%

commit v1 on v0

v1 whole, which is shorter than its diff:
```python
import functools
import numpy as np
import jax
import jax.numpy as jnp
from jax import lax
from jax.experimental import pallas as pl
from jax.experimental.pallas import tpu as pltpu
from jax.sharding import PartitionSpec as P

HD = 128
STEPS = 2
EPS = 1e-05
BASE = 500000.0
FLOOR = -1e30
SLOTS = 128
CAP = 4
MESH = pl.DeviceIdType.MESH
F32 = jnp.float32
BF16 = jnp.bfloat16


def iota(shape, axis):
    return lax.broadcasted_iota(jnp.int32, shape, axis)


def dot(a, b):
    return jnp.dot(a, b, preferred_element_type=F32)


def dot_t(a, b):
    return lax.dot_general(a, b, (((1,), (1,)), ((), ())), preferred_element_type=F32)


def to_row(column):
    n = column.shape[0]
    wide = jnp.broadcast_to(column, (n, n))
    return jnp.sum(jnp.where(iota((n, n), 0) == iota((n, n), 1), wide, 0.0), axis=0, keepdims=True)


def to_column(row):
    n = row.shape[1]
    wide = jnp.broadcast_to(row, (n, n))
    return jnp.sum(jnp.where(iota((n, n), 0) == iota((n, n), 1), wide, 0.0), axis=1, keepdims=True)


def angles(pos, freq):
    angle = pos * freq
    sign = jnp.where(iota(angle.shape, 1) < HD // 2, -1.0, 1.0)
    return jnp.cos(angle), jnp.sin(angle) * sign


def turn(vec, cosine, sine):
    return vec * cosine + pltpu.roll(vec, HD // 2, 1) * sine


def kernel(
    dims,
    hid_hbm, span_hbm, gain_hbm, wq_hbm, wkv_hbm, wo_hbm, cache_hbm, len_hbm, route_hbm, freq_hbm,
    out_ref,
    hid, span, gain, wq, wkvs, wkv, wo, cache, lens, route, freq,
    outbox, inbox, proj_out, proj_in, sq, heads_all, part_out, part_in, hid_all, qs, os_,
    load_sem, box_sem, proj_sem, sq_sem, heads_sem, part_sem, hid_sem,
):
    n_role, n_req, n_tp = dims
    role, req, tp = lax.axis_index("role"), lax.axis_index("req"), lax.axis_index("tp")
    owners = n_role * n_req
    me = role * n_req + req
    width = hid.shape[1]
    reqs = hid.shape[0]
    local = reqs // n_req
    ctx = cache.shape[1]
    heads = wq.shape[1] // HD
    rows_tp = reqs // n_tp

    def pool_peer(k):
        other = lax.rem(me + k, owners)
        return other, {"role": other // n_req, "req": lax.rem(other, n_req)}

    def req_peer(k):
        other = lax.rem(req + k, n_req)
        return other, {"req": other}

    def tp_peer(k):
        other = lax.rem(tp + k, n_tp)
        return other, {"tp": other}

    barrier = pltpu.get_barrier_semaphore()
    for k in range(1, owners):
        pl.semaphore_signal(barrier, inc=1, device_id=pool_peer(k)[1], device_id_type=MESH)
    for k in range(1, n_tp):
        pl.semaphore_signal(barrier, inc=1, device_id=tp_peer(k)[1], device_id_type=MESH)

    first = pl.multiple_of(req * width, width)
    loads = {}
    for index, (name, src, dst) in enumerate([
        ("hid", hid_hbm.at[0], hid),
        ("gain", gain_hbm, gain),
        ("wkvs", wkv_hbm.at[pl.ds(first, width)], wkvs),
        ("wq", wq_hbm, wq),
        ("route", route_hbm.at[0], route),
        ("freq", freq_hbm, freq),
        ("lens", len_hbm, lens),
        ("span", span_hbm.at[0], span),
        ("wkv", wkv_hbm, wkv),
        ("cache", cache_hbm.at[0], cache),
        ("wo", wo_hbm, wo),
    ]):
        loads[name] = pltpu.make_async_copy(src, dst, load_sem.at[index])
        loads[name].start()

    def exchange(peers, count, src, dst, send, recv):
        for k in peers:
            other, device = count(k)
            pltpu.make_async_remote_copy(
                src(other), dst, send, recv, device_id=device, device_id_type=MESH
            ).start()

    def wait_bytes(ref, send, recv, device):
        both = pltpu.make_async_remote_copy(ref, ref, send, recv, device_id=device, device_id_type=MESH)
        return both

    def project(rows, step, gain_row):
        wide = rows.astype(F32)
        squares = jnp.sum(wide * wide, axis=1, keepdims=True)
        sq[step, pl.ds(req, 1)] = to_row(squares).reshape(1, 1, reqs)
        mixed = (wide * gain_row).astype(BF16)
        both = jnp.concatenate([dot(mixed, wq[...]), dot(mixed, wkvs[...])], axis=1)
        both = both.reshape(n_req, local, -1)
        half = both.shape[2] // 2
        proj_out[step] = jnp.concatenate([both[:, :, :half], both[:, :, half:]], axis=1).astype(BF16)

    def send_projection(step):
        exchange(range(1, n_req), req_peer, lambda other: sq.at[step, req],
                 sq.at[step, req], sq_sem.at[step, 0], sq_sem.at[step, 1])
        exchange(range(1, n_req), req_peer, lambda other: proj_out.at[step, other],
                 proj_in.at[step, req], proj_sem.at[step, 0], proj_sem.at[step, 1])

    req_one, tp_one, pool_one = req_peer(1)[1], tp_peer(1)[1], pool_peer(1)[1]

    for name in ("hid", "gain", "wkvs", "wq"):
        loads[name].wait()
    gains = gain[...].astype(F32)
    gain_row = jnp.sum(jnp.where(iota(gains.shape, 0) == req, gains, 0.0), axis=0, keepdims=True)
    project(hid[...], 0, gain_row)
    pl.semaphore_wait(barrier, owners + n_tp - 2)
    send_projection(0)

    for name in ("route", "freq", "lens", "span", "wkv"):
        loads[name].wait()
    count = span.shape[0]
    freq_row = freq[0:1, :]
    acc = jnp.zeros((count, 2 * HD), F32)
    squares = jnp.zeros((count, 1), F32)
    for j in range(n_req):
        wide = span[:, j * width:(j + 1) * width].astype(F32)
        squares += jnp.sum(wide * wide, axis=1, keepdims=True)
        acc += dot((wide * gains[j:j + 1, :]).astype(BF16), wkv[j * width:(j + 1) * width, :])
    keyval = acc * lax.rsqrt(squares / (n_req * width) + EPS)
    plan = route[...]
    owner = plan[:, 0:1].astype(F32)
    slot = plan[:, 2:3].astype(F32)
    cosine, sine = angles(slot, freq_row)
    key = turn(keyval[:, :HD], cosine, sine).astype(BF16)
    value = keyval[:, HD:].astype(BF16)
    owner_row = to_row(owner)
    square = (count, count)
    earlier = (iota(square, 0) < iota(square, 1)) & (
        jnp.broadcast_to(owner, square) == jnp.broadcast_to(owner_row, square))
    rank_row = jnp.sum(jnp.where(earlier, 1.0, 0.0), axis=0, keepdims=True)
    place = (owner_row * (4 * CAP) + rank_row).astype(jnp.int32)
    lines = iota((owners * 4 * CAP, count), 0)
    ask = jnp.broadcast_to(plan[:, 1:2].astype(F32) + 1.0, (count, HD)).astype(BF16)
    spot = jnp.broadcast_to(slot, (count, HD)).astype(BF16)
    box = jnp.zeros((owners * 4 * CAP, HD), F32)
    for part, content in enumerate((key, value, ask, spot)):
        pick = jnp.where(lines == place + part * CAP, 1.0, 0.0).astype(BF16)
        box += dot(pick, content)
    outbox[...] = box.astype(BF16)
    chunk = 4 * CAP
    mine = pl.ds(pl.multiple_of(me * chunk, chunk), chunk)
    inbox[mine] = outbox[mine]
    exchange(range(1, owners), pool_peer,
             lambda other: outbox.at[pl.ds(pl.multiple_of(other * chunk, chunk), chunk)],
             inbox.at[mine], box_sem.at[0], box_sem.at[1])

    len_row = lens[...].astype(F32)
    len_col = to_column(len_row)
    tables = [angles(len_col + float(step), freq_row) for step in range(STEPS)]
    pick = (local * heads, local)
    len_rows = jnp.sum(
        jnp.where(iota(pick, 0) // heads == iota(pick, 1),
                  jnp.broadcast_to(len_row, pick), 0.0), axis=1, keepdims=True)

    loads["cache"].wait()
    box_wait = wait_bytes(inbox.at[pl.ds(0, (owners - 1) * chunk)], box_sem.at[0], box_sem.at[1], pool_one)
    box_wait.wait_recv()
    arrived = inbox[...]
    total = owners * CAP
    sel = (4 * total, owners * chunk)
    line = iota(sel, 0)
    part = line // total
    item = lax.rem(line, total)
    want = (item // CAP) * chunk + part * CAP + lax.rem(item, CAP)
    sorted_ = dot(jnp.where(iota(sel, 1) == want, 1.0, 0.0).astype(BF16), arrived)
    key_in = sorted_[0:total].astype(BF16)
    value_in = sorted_[total:2 * total].astype(BF16)
    target = (sorted_[2 * total:3 * total] - 1.0) * float(SLOTS) + sorted_[3 * total:]
    target = jnp.where(sorted_[2 * total:3 * total] > 0.5, target, -1.0)
    target_row = to_row(target[:, 0:1]).astype(jnp.int32)
    ones = jnp.ones((total, HD), BF16)
    for b in range(local):
        hot = jnp.where(iota((SLOTS, total), 0) + b * SLOTS == target_row, 1.0, 0.0).astype(BF16)
        hit = dot(hot, ones) > 0.5
        for lo, rows in ((0, key_in), (HD, value_in)):
            old = cache[b, 0:SLOTS, lo:lo + HD]
            cache[b, 0:SLOTS, lo:lo + HD] = jnp.where(hit, dot(hot, rows), old.astype(F32)).astype(BF16)

    hidden = hid[...]
    fresh = []
    inverse = HD ** (-0.5)
    for step in range(STEPS):
        if step > 0:
            project(hidden, step, gain_row)
            send_projection(step)
        sq_wait = wait_bytes(sq.at[step, pl.ds(0, n_req - 1)], sq_sem.at[step, 0], sq_sem.at[step, 1], req_one)
        proj_wait = wait_bytes(
            proj_in.at[step, pl.ds(0, n_req - 1)], proj_sem.at[step, 0], proj_sem.at[step, 1], req_one)
        proj_in[step, pl.ds(req, 1)] = proj_out[step, pl.ds(req, 1)]
        sq_wait.wait_recv()
        all_squares = jnp.sum(sq[step].reshape(n_req, reqs), axis=0, keepdims=True)
        grid = (local, reqs)
        own = jnp.sum(
            jnp.where(iota(grid, 1) == iota(grid, 0) + req * local,
                      jnp.broadcast_to(all_squares, grid), 0.0), axis=1, keepdims=True)
        scale = lax.rsqrt(own / (n_req * width) + EPS)
        proj_wait.wait_recv()
        summed = proj_in[step, 0].astype(F32)
        for k in range(1, n_req):
            summed += proj_in[step, k].astype(F32)
        half = summed.shape[1]
        flat = jnp.concatenate([summed[:local], summed[local:]], axis=1) * scale
        cosine, sine = tables[step]
        for h in range(heads):
            qs[pl.ds(h, local, stride=heads), :] = turn(flat[:, h * HD:(h + 1) * HD], cosine, sine)
        base = heads * HD
        fresh_key = turn(flat[:, base:base + HD], cosine, sine).astype(BF16).astype(F32)
        fresh_value = flat[:, base + HD:].astype(BF16).astype(F32)
        fresh.append((fresh_key, fresh_value))
        for b in range(local):
            query = qs[b * heads:(b + 1) * heads, :].astype(BF16)
            wide = query.astype(F32)
            news = [
                jnp.sum(wide * k[b:b + 1, :], axis=1, keepdims=True) * inverse for k, _ in fresh
            ]
            old = dot_t(query, cache[b, :, 0:HD]) * inverse
            live = iota((heads, ctx), 1).astype(F32) < len_rows[b * heads:(b + 1) * heads]
            old = jnp.where(live, old, FLOOR)
            top = jnp.max(old, axis=1, keepdims=True)
            for new in news:
                top = jnp.maximum(top, new)
            old_exp = jnp.where(live, jnp.exp(old - top), 0.0)
            new_exp = [jnp.exp(new - top) for new in news]
            norm = jnp.sum(old_exp, axis=1, keepdims=True)
            for item in new_exp:
                norm += item
            mixture = dot(old_exp.astype(BF16), cache[b, :, HD:])
            for item, (_, v) in zip(new_exp, fresh):
                mixture += item.astype(BF16).astype(F32) * v[b:b + 1, :]
            os_[b * heads:(b + 1) * heads, :] = mixture / norm
        pieces = [os_[pl.ds(h, local, stride=heads), :] for h in range(heads)]
        mid = heads // 2
        block = jnp.concatenate(
            [jnp.concatenate(pieces[:mid], axis=1), jnp.concatenate(pieces[mid:], axis=1)], axis=0)
        heads_all[step, pl.ds(req, 1)] = block.astype(BF16).reshape(1, 2 * local, mid * HD)
        exchange(range(1, n_req), req_peer, lambda other: heads_all.at[step, req],
                 heads_all.at[step, req], heads_sem.at[step, 0], heads_sem.at[step, 1])
        if step == 0:
            loads["wo"].wait()
        heads_wait = wait_bytes(
            heads_all.at[step, pl.ds(0, n_req - 1)], heads_sem.at[step, 0], heads_sem.at[step, 1], req_one)
        heads_wait.wait_recv()
        left = heads_all[step].reshape(n_req * 2 * local, mid * HD)
        upper = dot(left, wo[:mid * HD, :]).reshape(n_req, 2 * local, width)
        lower = dot(left, wo[mid * HD:, :]).reshape(n_req, 2 * local, width)
        partial = (upper[:, :local] + lower[:, local:]).reshape(n_tp, rows_tp, width)
        part_out[step] = partial.astype(BF16)
        exchange(range(1, n_tp), tp_peer, lambda other: part_out.at[step, other],
                 part_in.at[step, tp], part_sem.at[step, 0], part_sem.at[step, 1])
        part_in[step, pl.ds(tp, 1)] = part_out[step, pl.ds(tp, 1)]
        part_wait = wait_bytes(
            part_in.at[step, pl.ds(0, n_tp - 1)], part_sem.at[step, 0], part_sem.at[step, 1], tp_one)
        part_wait.wait_recv()
        rows = pl.ds(pl.multiple_of(tp * rows_tp, rows_tp), rows_tp)
        before = hid[rows, :] if step == 0 else hid_all[rows, :]
        summed = part_in[step, 0].astype(F32)
        for k in range(1, n_tp):
            summed += part_in[step, k].astype(F32)
        after = (before.astype(F32) + summed).astype(BF16)
        if step < STEPS - 1:
            dst = hid_all
            hid_all[rows, :] = after
        else:
            dst = out_ref.at[0]
            out_ref[0, rows, :] = after
        exchange(range(1, n_tp), tp_peer, lambda other: dst.at[rows], dst.at[rows],
                 hid_sem.at[step, 0], hid_sem.at[step, 1])
        hid_wait = wait_bytes(
            dst.at[pl.ds(0, (n_tp - 1) * rows_tp)], hid_sem.at[step, 0], hid_sem.at[step, 1], tp_one)
        hid_wait.wait_recv()
        if step < STEPS - 1:
            hidden = hid_all[...]
        for item in (sq_wait, proj_wait, heads_wait, part_wait, hid_wait):
            item.wait_send()
    box_wait.wait_send()


def on_device(dims, decode_hidden, span_hidden, norm_gain, w_query, w_keyval, w_out, cache, lengths, route):
    n_role, n_req, n_tp = dims
    owners = n_role * n_req
    _, reqs, width = decode_hidden.shape
    _, count, _ = span_hidden.shape
    local = reqs // n_req
    cols = w_query.shape[1] + w_keyval.shape[1]
    heads = w_query.shape[1] // HD
    half = HD // 2
    table = np.power(np.float32(BASE), -np.arange(half, dtype=np.float32) / np.float32(half))
    freq = jnp.asarray(np.tile(table.astype(np.float32), (8, 2)))
    any_spec = pl.BlockSpec(memory_space=pl.ANY)
    vmem = pltpu.VMEM
    sems = pltpu.SemaphoreType.DMA
    return pl.pallas_call(
        functools.partial(kernel, dims),
        out_shape=jax.ShapeDtypeStruct(decode_hidden.shape, BF16),
        in_specs=[any_spec] * 10,
        out_specs=pl.BlockSpec(memory_space=pltpu.VMEM),
        scratch_shapes=[
            vmem((reqs, width), BF16),
            vmem(span_hidden.shape[1:], BF16),
            vmem((n_req, width), BF16),
            vmem(w_query.shape, BF16),
            vmem((width, w_keyval.shape[1]), BF16),
            vmem(w_keyval.shape, BF16),
            vmem(w_out.shape, BF16),
            vmem(cache.shape[1:], BF16),
            vmem(lengths.shape, jnp.int32),
            vmem(route.shape[1:], jnp.int32),
            vmem(freq.shape, F32),
            vmem((owners * 4 * CAP, HD), BF16),
            vmem((owners * 4 * CAP, HD), BF16),
            vmem((STEPS, n_req, 2 * local, cols // 2), BF16),
            vmem((STEPS, n_req, 2 * local, cols // 2), BF16),
            vmem((STEPS, n_req, 1, reqs), F32),
            vmem((STEPS, n_req, 2 * local, heads * HD // 2), BF16),
            vmem((STEPS, n_tp, reqs // n_tp, width), BF16),
            vmem((STEPS, n_tp, reqs // n_tp, width), BF16),
            vmem((reqs, width), BF16),
            vmem((local * heads, HD), F32),
            vmem((local * heads, HD), F32),
            sems((11,)),
            sems((2,)),
            sems((STEPS, 2)),
            sems((STEPS, 2)),
            sems((STEPS, 2)),
            sems((STEPS, 2)),
            sems((STEPS, 2)),
        ],
        compiler_params=pltpu.CompilerParams(
            collective_id=0, has_side_effects=True, vmem_limit_bytes=56 * 2**20
        ),
        name="decode",
    )(decode_hidden, span_hidden, norm_gain.reshape(n_req, width), w_query, w_keyval, w_out, cache,
      lengths, route, freq)


def solution(mesh):
    dims = tuple(mesh.shape[name] for name in ("role", "req", "tp"))
    placed = (
        P("role", None, "req"),
        P("role", "req", None),
        P(),
        P("req", "tp"),
        P(None, "tp"),
        P("tp", "req"),
        P("role", "req", None, "tp"),
        P("role", "req"),
        P("role", "req", None),
    )
    return jax.shard_map(
        functools.partial(on_device, dims), mesh=mesh, in_specs=placed,
        out_specs=P("role", None, "req"), check_vma=False,
    )
```

time: 432 us -> 71.4 us (0.17)
  waiting for transfers between devices: 231 us -> 0 us
  blocking collectives: 108 us -> 0 us
  Pallas kernels: 0 us -> 67 us
  local copies, waits for them, and re-layouts: 31.7 us -> 4.28 us
  starting transfers between devices: 19.3 us -> 0 us
  matrix products: 17.3 us -> 0 us
  between operations: 14.2 us -> 0.01 us
  other arithmetic: 8.59 us -> 0 us
    psum x2 -> x0, waiting for transfers between devices: 146 us -> none  [decode_step(): total = lax.psum(partial_value, 'tp')]
    unnamed x6 -> x0, waiting for transfers between devices: 80.3 us -> none
    pallas_call x0 -> x1, Pallas kernels: none -> 67 us  [on_device(): pl.pallas_call(functools.partial(kernel, dims), out_shape=jax.ShapeDtypeS...]
    psum x2 -> x0, blocking collectives: 65 us -> none  [decode_step(): squares = lax.psum(local_squares, 'req')]
    all_gather x2 -> x0, blocking collectives: 43.4 us -> none  [decode_step(): lax.all_gather(heads, 'req', axis=0, tiled=True)]
    scatter x4 -> x0, local copies, waits for them, and re-layouts: 24.1 us -> none  [the longest x2 22.5 us: on_device(): cache_own = cache[0].at[request, target].set(inbox, mode='drop')]
    all_to_all x2 -> x0, starting transfers between devices: 19.1 us -> none  [the longest x1 11.8 us: on_device(): lax.all_to_all(outbox.reshape(owners, limit, -1), ('role', 'req'), split_...]
    dot_general x14 -> x0, matrix products: 17.3 us -> none  [the longest x2 4.57 us: attend_block(): jnp.einsum('rgjc,rcgd->rgjd', weight_old, values, preferred_element_type=...]
  transfers between devices with their start and end apart: 6 -> 0, of which waited for: 5 -> 0; matrix products, arithmetic and copies ran while one was open for 7% -> 0% of each run, Pallas kernels for 0% -> 0%
where the time goes in v1:
time: 71.4 us; the launch traced here: 71.2 us
  Pallas kernels  67 us (94%)
  local copies, waits for them, and re-layouts  4.28 us (6%)
    pallas_call x1, Pallas kernels, on_device(): pl.pallas_call(functools.partial(kernel, dims), out_shape=jax.ShapeDtypeS...  67 us
    unnamed x2, local copies, waits for them, and re-layouts  2.95 us

profile of v1, /device:TPU:24, one launch (start us, length us, event | category | flops | bytes accessed | tf_op | source)
XLA Modules:
  0.0 71.2 jit_solution(7284017173126366044)
XLA Ops:
  0.0 1.3 %reshape.3.gain_hbm = bf16[16,512]{1,0:T(8,128)(2,1)} reshape(bf16[8192]{0:T(1024)(128)(2,1)} %param.12) | data formatting | bytes 32768 | tf_op jit(solution)/shard_map/reshape | solution.py:371
  1.3 1.4 %copy.11.route_hbm = s32[1,64,3]{2,1,0:T(8,128)} copy(s32[1,64,3]{1,0,2:T(1,128)} %param.18) | data formatting | bytes 1536 | tf_op args[8]
  2.7 67.0 %decode.1 = bf16[1,128,512]{2,1,0:T(8,128)(2,1)} custom-call(bf16[1,128,512]{2,1,0:T(8,128)(2,1)} %hid_hbm.1, bf16[1,64,8192]{2,1,0:T(8,128)(2,1)} %span_hbm.1, bf16[16,512]{1,0:T(8,128)(2,1)} %reshape.3.gain_hbm, bf16[512,1024]{1,0:T(8,128)(2,1)} %wq_hbm.1, bf16[8192,256]{1,0:T(8,128)(2,1)} %wkv_hbm.1, bf16[1024,512]{1,0:T(8,128)(2,1)} %wo_hbm.1, ...), custom_call_target="tpu_custom_call" | custom-call | tf_op jit(solution)/shard_map/decode/pallas_call | solution.py:331
  69.7 1.6 %copy.13 = bf16[1,128,512]{2,1,0:T(8,128)(2,1)} copy(bf16[1,128,512]{2,1,0:T(8,128)(2,1)} %decode.1) | data formatting | bytes 262144

commit v2 on v1

v2 whole, which is shorter than its diff:
```python
import functools
import numpy as np
import jax
import jax.numpy as jnp
from jax import lax
from jax.experimental import pallas as pl
from jax.experimental.pallas import tpu as pltpu
from jax.sharding import PartitionSpec as P

HD = 128
STEPS = 2
EPS = 1e-05
BASE = 500000.0
FLOOR = -1e30
SLOTS = 128
CAP = 4
MESH = pl.DeviceIdType.MESH
F32 = jnp.float32
BF16 = jnp.bfloat16


def iota(shape, axis):
    return lax.broadcasted_iota(jnp.int32, shape, axis)


def dot(a, b):
    return jnp.dot(a, b, preferred_element_type=F32)


def dot_t(a, b):
    return lax.dot_general(a, b, (((1,), (1,)), ((), ())), preferred_element_type=F32)


def to_row(column):
    n = column.shape[0]
    wide = jnp.broadcast_to(column, (n, n))
    return jnp.sum(jnp.where(iota((n, n), 0) == iota((n, n), 1), wide, 0.0), axis=0, keepdims=True)


def to_column(row):
    n = row.shape[1]
    wide = jnp.broadcast_to(row, (n, n))
    return jnp.sum(jnp.where(iota((n, n), 0) == iota((n, n), 1), wide, 0.0), axis=1, keepdims=True)


def angles(pos, freq):
    angle = pos * freq
    sign = jnp.where(iota(angle.shape, 1) < HD // 2, -1.0, 1.0)
    return jnp.cos(angle), jnp.sin(angle) * sign


def turn(vec, cosine, sine):
    return vec * cosine + pltpu.roll(vec, HD // 2, 1) * sine


def kernel(
    dims,
    hid_hbm, span_hbm, gain_hbm, wq_hbm, wkv_hbm, wo_hbm, cache_hbm, len_hbm, route_hbm, freq_hbm,
    out_ref,
    hid, span, gain, wq, wkvs, wkv, wo, cache, lens, route, freq,
    outbox, inbox, proj_out, proj_in, heads_all, part_out, part_in, hid_all, qs, os_,
    load_sem, box_sem, proj_sem, heads_sem, part_sem, hid_sem,
):
    n_role, n_req, n_tp = dims
    role, req, tp = lax.axis_index("role"), lax.axis_index("req"), lax.axis_index("tp")
    owners = n_role * n_req
    me = role * n_req + req
    width = hid.shape[1]
    reqs = hid.shape[0]
    local = reqs // n_req
    ctx = cache.shape[1]
    heads = wq.shape[1] // HD
    rows_tp = reqs // n_tp

    side = int(n_req ** 0.5)

    def far(k, n):
        return min(k, n - k)

    steps = [(a, b) for a in range(side) for b in range(side)]
    steps.sort(key=lambda s: -far(s[0], side) - far(s[1], side))
    req_steps = steps[:-1]
    pool_steps = [(flip, s) for s in steps for flip in (False, True)]
    pool_steps.remove((False, (0, 0)))
    tp_steps = sorted(range(1, n_tp), key=lambda k: -far(k, n_tp))

    def req_peer(step, flip=False):
        other = lax.rem(req // side + step[0], side) * side + lax.rem(lax.rem(req, side) + step[1], side)
        return other, {"role": 1 - role if flip else role, "req": other}

    def pool_peer(step):
        other, device = req_peer(step[1], step[0])
        return device["role"] * n_req + other, device

    def tp_peer(k):
        other = lax.rem(tp + k, n_tp)
        return other, {"tp": other}

    first = pl.multiple_of(req * width, width)
    loads = {}
    arrays = [
        ("hid", hid_hbm.at[0], hid),
        ("gain", gain_hbm, gain),
        ("wkvs", wkv_hbm.at[pl.ds(first, width)], wkvs),
        ("wq", wq_hbm, wq),
        ("route", route_hbm, route),
        ("freq", freq_hbm, freq),
        ("lens", len_hbm, lens),
        ("span", span_hbm.at[0], span),
        ("wkv", wkv_hbm, wkv),
        ("cache", cache_hbm.at[0], cache),
        ("wo", wo_hbm, wo),
    ]

    def load(some):
        for index in some:
            name, src, dst = arrays[index]
            loads[name] = pltpu.make_async_copy(src, dst, load_sem.at[index])
            loads[name].start()

    load(range(4))
    barrier = pltpu.get_barrier_semaphore()
    greeted = [pool_peer(k)[1] for k in pool_steps]
    greeted += [tp_peer(k)[1] for k in tp_steps]
    for device in greeted:
        pl.semaphore_signal(barrier, inc=1, device_id=device, device_id_type=MESH)
    load(range(4, len(arrays)))

    def exchange(peers, peer, src, dst, sems):
        for k in peers:
            other, device = peer(k)
            pltpu.make_async_remote_copy(
                src(other), dst, sems.at[0], sems.at[1], device_id=device, device_id_type=MESH
            ).start()

    def arrivals(ref, sems):
        return pltpu.make_async_remote_copy(
            ref, ref, sems.at[0], sems.at[1], device_id=req_peer(steps[0])[1], device_id_type=MESH
        )

    def project(rows, step, gain_row):
        wide = rows.astype(F32)
        squares = jnp.sum(wide * wide, axis=1, keepdims=True)
        squares = jnp.broadcast_to(squares, (reqs, HD)).reshape(n_req, local, HD)
        main = squares.astype(BF16).astype(F32)
        mixed = (wide * gain_row).astype(BF16)
        both = jnp.concatenate([dot(mixed, wq[...]), dot(mixed, wkvs[...])], axis=1)
        both = both.reshape(n_req, local, -1)
        half = both.shape[2] // 2
        upper = jnp.concatenate([both[:, :, :half], main], axis=2)
        lower = jnp.concatenate([both[:, :, half:], squares - main], axis=2)
        proj_out[step] = jnp.concatenate([upper, lower], axis=1).astype(BF16)

    def send_projection(step):
        exchange(req_steps, req_peer, lambda other: proj_out.at[step, other],
                 proj_in.at[step, req], proj_sem.at[step])

    for name in ("hid", "gain", "wkvs", "wq"):
        loads[name].wait()
    gains = jnp.concatenate(
        [gain[j * width:(j + 1) * width].astype(F32).reshape(1, width) for j in range(n_req)], axis=0)
    gain_row = jnp.sum(jnp.where(iota(gains.shape, 0) == req, gains, 0.0), axis=0, keepdims=True)
    project(hid[...], 0, gain_row)
    pl.semaphore_wait(barrier, len(greeted))
    send_projection(0)

    for name in ("route", "freq", "lens", "span", "wkv"):
        loads[name].wait()
    count = span.shape[0]
    freq_row = freq[0:1, :]
    acc = jnp.zeros((count, 2 * HD), F32)
    squares = jnp.zeros((count, 1), F32)
    for j in range(n_req):
        wide = span[:, j * width:(j + 1) * width].astype(F32)
        squares += jnp.sum(wide * wide, axis=1, keepdims=True)
        acc += dot((wide * gains[j:j + 1, :]).astype(BF16), wkv[j * width:(j + 1) * width, :])
    keyval = acc * lax.rsqrt(squares / (n_req * width) + EPS)
    owner_row, ask, slot = (route[j].astype(F32) for j in range(3))
    owner, ask, slot = to_column(owner_row), to_column(ask), to_column(slot)
    cosine, sine = angles(slot, freq_row)
    key = turn(keyval[:, :HD], cosine, sine).astype(BF16)
    value = keyval[:, HD:].astype(BF16)
    square = (count, count)
    earlier = (iota(square, 0) < iota(square, 1)) & (
        jnp.broadcast_to(owner, square) == jnp.broadcast_to(owner_row, square))
    rank_row = jnp.sum(jnp.where(earlier, 1.0, 0.0), axis=0, keepdims=True)
    place = (owner_row * (4 * CAP) + rank_row).astype(jnp.int32)
    lines = iota((owners * 4 * CAP, count), 0)
    ask = jnp.broadcast_to(ask + 1.0, (count, HD)).astype(BF16)
    spot = jnp.broadcast_to(slot, (count, HD)).astype(BF16)
    box = jnp.zeros((owners * 4 * CAP, HD), F32)
    for part, content in enumerate((key, value, ask, spot)):
        pick = jnp.where(lines == place + part * CAP, 1.0, 0.0).astype(BF16)
        box += dot(pick, content)
    outbox[...] = box.astype(BF16)
    chunk = 4 * CAP
    mine = pl.ds(pl.multiple_of(me * chunk, chunk), chunk)
    inbox[mine] = outbox[mine]
    exchange(pool_steps, pool_peer,
             lambda other: outbox.at[pl.ds(pl.multiple_of(other * chunk, chunk), chunk)],
             inbox.at[mine], box_sem)

    len_row = lens[...].astype(F32)
    len_col = to_column(len_row)
    tables = [angles(len_col + float(step), freq_row) for step in range(STEPS)]
    pick = (local * heads, local)
    len_rows = jnp.sum(
        jnp.where(iota(pick, 0) // heads == iota(pick, 1),
                  jnp.broadcast_to(len_row, pick), 0.0), axis=1, keepdims=True)

    def place_handed():
        arrived = inbox[...]
        total = owners * CAP
        sel = (4 * total, owners * chunk)
        line = iota(sel, 0)
        part = line // total
        item = lax.rem(line, total)
        want = (item // CAP) * chunk + part * CAP + lax.rem(item, CAP)
        sorted_ = dot(jnp.where(iota(sel, 1) == want, 1.0, 0.0).astype(BF16), arrived)
        key_in = sorted_[0:total].astype(BF16)
        value_in = sorted_[total:2 * total].astype(BF16)
        target = (sorted_[2 * total:3 * total] - 1.0) * float(SLOTS) + sorted_[3 * total:]
        target = jnp.where(sorted_[2 * total:3 * total] > 0.5, target, -1.0)
        target_row = to_row(target[:, 0:1]).astype(jnp.int32)
        ones = jnp.ones((total, HD), BF16)
        for b in range(local):
            hot = jnp.where(iota((SLOTS, total), 0) + b * SLOTS == target_row, 1.0, 0.0).astype(BF16)
            hit = dot(hot, ones) > 0.5
            for lo, rows in ((0, key_in), (HD, value_in)):
                old = cache[b, 0:SLOTS, lo:lo + HD]
                cache[b, 0:SLOTS, lo:lo + HD] = jnp.where(hit, dot(hot, rows), old.astype(F32)).astype(BF16)

    loads["cache"].wait()
    box_wait = arrivals(inbox.at[pl.ds(0, (owners - 1) * chunk)], box_sem)
    sent = [box_wait]
    fresh = []
    inverse = HD ** (-0.5)
    many = local * heads
    hidden = hid
    for step in range(STEPS):
        last = step == STEPS - 1
        if step > 0:
            project(hidden[...], step, gain_row)
            send_projection(step)
        proj_wait = arrivals(proj_in.at[step, pl.ds(0, n_req - 1)], proj_sem.at[step])
        proj_in[step, pl.ds(req, 1)] = proj_out[step, pl.ds(req, 1)]
        proj_wait.wait_recv()
        summed = proj_in[step, 0].astype(F32)
        for k in range(1, n_req):
            summed += proj_in[step, k].astype(F32)
        half = summed.shape[1] - HD
        own = summed[:local, half:half + 1] + summed[local:, half:half + 1]
        scale = lax.rsqrt(own / (n_req * width) + EPS)
        flat = jnp.concatenate([summed[:local, :half], summed[local:, :half]], axis=1) * scale
        cosine, sine = tables[step]
        for h in range(heads):
            qs[pl.ds(h, local, stride=heads), :] = turn(flat[:, h * HD:(h + 1) * HD], cosine, sine)
        base = heads * HD

        def spread(rows):
            rows = rows.astype(BF16).astype(F32)
            return jnp.broadcast_to(rows[:, None, :], (local, heads, HD)).reshape(many, HD)

        fresh.append((spread(turn(flat[:, base:base + HD], cosine, sine)), spread(flat[:, base + HD:])))
        queries = [qs[b * heads:(b + 1) * heads, :].astype(BF16) for b in range(local)]

        def scores(lo, hi):
            return jnp.concatenate(
                [dot_t(queries[b], cache[b, lo:hi, 0:HD]) for b in range(local)], axis=0) * inverse

        late = scores(SLOTS, ctx)
        live = iota(late.shape, 1) + SLOTS < len_rows
        late = jnp.where(live, late, FLOOR)
        if step == 0:
            box_wait.wait_recv()
            place_handed()
        early = scores(0, SLOTS)
        wide = qs[...].astype(BF16).astype(F32)
        news = [jnp.sum(wide * k, axis=1, keepdims=True) * inverse for k, _ in fresh]
        top = jnp.maximum(jnp.max(late, axis=1, keepdims=True), jnp.max(early, axis=1, keepdims=True))
        for new in news:
            top = jnp.maximum(top, new)
        early, late = jnp.exp(early - top), jnp.exp(late - top)
        norm = jnp.sum(early, axis=1, keepdims=True) + jnp.sum(late, axis=1, keepdims=True)
        weights = jnp.concatenate([early, late], axis=1)
        mixture = jnp.concatenate([
            dot(weights[b * heads:(b + 1) * heads].astype(BF16), cache[b, :, HD:]) for b in range(local)
        ], axis=0)
        for new, (_, v) in zip(news, fresh):
            new = jnp.exp(new - top)
            norm += new
            mixture += new.astype(BF16).astype(F32) * v
        os_[...] = mixture / norm
        pieces = [os_[pl.ds(h, local, stride=heads), :] for h in range(heads)]
        mid = heads // 2
        block = jnp.concatenate(
            [jnp.concatenate(pieces[:mid], axis=1), jnp.concatenate(pieces[mid:], axis=1)], axis=0)
        heads_all[step, pl.ds(req, 1)] = block.astype(BF16).reshape(1, 2 * local, mid * HD)
        exchange(req_steps, req_peer, lambda other: heads_all.at[step, req],
                 heads_all.at[step, req], heads_sem.at[step])
        if step == 0:
            loads["wo"].wait()
        heads_wait = arrivals(heads_all.at[step, pl.ds(0, n_req - 1)], heads_sem.at[step])
        heads_wait.wait_recv()
        left = heads_all[step].reshape(n_req * 2 * local, mid * HD)
        upper = dot(left, wo[:mid * HD, :]).reshape(n_req, 2 * local, width)
        lower = dot(left, wo[mid * HD:, :]).reshape(n_req, 2 * local, width)
        partial = (upper[:, :local] + lower[:, local:]).reshape(n_tp, rows_tp, width)
        part_out[step] = partial.astype(BF16)
        exchange(tp_steps, tp_peer, lambda other: part_out.at[step, other],
                 part_in.at[step, tp], part_sem.at[step])
        part_in[step, pl.ds(tp, 1)] = part_out[step, pl.ds(tp, 1)]
        part_wait = arrivals(part_in.at[step, pl.ds(0, n_tp - 1)], part_sem.at[step])
        part_wait.wait_recv()
        rows = pl.ds(pl.multiple_of(tp * rows_tp, rows_tp), rows_tp)
        summed = hidden[rows, :].astype(F32)
        for k in range(n_tp):
            summed += part_in[step, k].astype(F32)
        target = out_ref.at[0] if last else hid_all
        target[rows, :] = summed.astype(BF16)
        exchange(tp_steps, tp_peer, lambda other: target.at[rows], target.at[rows], hid_sem.at[step])
        hid_wait = arrivals(target.at[pl.ds(0, (n_tp - 1) * rows_tp)], hid_sem.at[step])
        hid_wait.wait_recv()
        hidden = hid_all
        sent += [proj_wait, heads_wait, part_wait, hid_wait]
    for item in sent:
        item.wait_send()


def on_device(dims, decode_hidden, span_hidden, norm_gain, w_query, w_keyval, w_out, cache, lengths, route):
    n_role, n_req, n_tp = dims
    owners = n_role * n_req
    _, reqs, width = decode_hidden.shape
    _, count, _ = span_hidden.shape
    local = reqs // n_req
    cols = w_query.shape[1] + w_keyval.shape[1]
    heads = w_query.shape[1] // HD
    half = HD // 2
    table = np.power(np.float32(BASE), -np.arange(half, dtype=np.float32) / np.float32(half))
    freq = jnp.asarray(np.tile(table.astype(np.float32), (8, 2)))
    any_spec = pl.BlockSpec(memory_space=pl.ANY)
    vmem = pltpu.VMEM
    sems = pltpu.SemaphoreType.DMA
    return pl.pallas_call(
        functools.partial(kernel, dims),
        out_shape=pltpu.VMEM(decode_hidden.shape, BF16),
        in_specs=[any_spec] * 10,
        out_specs=pl.BlockSpec(memory_space=pltpu.VMEM),
        scratch_shapes=[
            vmem((reqs, width), BF16),
            vmem(span_hidden.shape[1:], BF16),
            vmem(norm_gain.shape, BF16),
            vmem(w_query.shape, BF16),
            vmem((width, w_keyval.shape[1]), BF16),
            vmem(w_keyval.shape, BF16),
            vmem(w_out.shape, BF16),
            vmem(cache.shape[1:], BF16),
            vmem(lengths.shape, jnp.int32),
            vmem((3, 1, count), jnp.int32),
            vmem(freq.shape, F32),
            vmem((owners * 4 * CAP, HD), BF16),
            vmem((owners * 4 * CAP, HD), BF16),
            vmem((STEPS, n_req, 2 * local, cols // 2 + HD), BF16),
            vmem((STEPS, n_req, 2 * local, cols // 2 + HD), BF16),
            vmem((STEPS, n_req, 2 * local, heads * HD // 2), BF16),
            vmem((STEPS, n_tp, reqs // n_tp, width), BF16),
            vmem((STEPS, n_tp, reqs // n_tp, width), BF16),
            vmem((reqs, width), BF16),
            vmem((local * heads, HD), F32),
            vmem((local * heads, HD), F32),
            sems((11,)),
            sems((2,)),
            sems((STEPS, 2)),
            sems((STEPS, 2)),
            sems((STEPS, 2)),
            sems((STEPS, 2)),
        ],
        compiler_params=pltpu.CompilerParams(
            collective_id=0, has_side_effects=True, vmem_limit_bytes=56 * 2**20
        ),
        name="decode",
    )(decode_hidden, span_hidden, norm_gain, w_query, w_keyval, w_out, cache,
      lengths, jnp.transpose(route, (2, 0, 1)), freq)


def solution(mesh):
    dims = tuple(mesh.shape[name] for name in ("role", "req", "tp"))
    placed = (
        P("role", None, "req"),
        P("role", "req", None),
        P(),
        P("req", "tp"),
        P(None, "tp"),
        P("tp", "req"),
        P("role", "req", None, "tp"),
        P("role", "req"),
        P("role", "req", None),
    )
    return jax.shard_map(
        functools.partial(on_device, dims), mesh=mesh, in_specs=placed,
        out_specs=P("role", None, "req"), check_vma=False,
    )
```

time: 71.4 us -> 60 us (0.84)
  Pallas kernels: 67 us -> 59.1 us
  local copies, waits for them, and re-layouts: 4.28 us -> 0.66 us
    pallas_call x1, Pallas kernels: 67 us -> 59.1 us  [on_device(): pl.pallas_call(functools.partial(kernel, dims), out_shape=pltpu.VMEM(deco...]
    unnamed x2 -> x1, local copies, waits for them, and re-layouts: 2.95 us -> 0.66 us
    reshape x1 -> x0, local copies, waits for them, and re-layouts: 1.33 us -> none  [on_device(): norm_gain.reshape(n_req, width)]
where the time goes in v2:
time: 60 us; the launch traced here: 59.8 us
  Pallas kernels  59.1 us (98%)
  local copies, waits for them, and re-layouts  0.66 us (1%)
    pallas_call x1, Pallas kernels, on_device(): pl.pallas_call(functools.partial(kernel, dims), out_shape=pltpu.VMEM(deco...  59.1 us

profile of v2, /device:TPU:24, one launch (start us, length us, event | category | flops | bytes accessed | tf_op | source)
XLA Modules:
  0.0 59.8 jit_solution(12302748425576558614)
XLA Ops:
  0.0 59.1 %decode.1 = bf16[1,128,512]{2,1,0:T(8,128)(2,1)S(1)} custom-call(bf16[1,128,512]{2,1,0:T(8,128)(2,1)} %hid_hbm.1, bf16[1,64,8192]{2,1,0:T(8,128)(2,1)} %span_hbm.1, bf16[8192]{0:T(1024)(128)(2,1)} %gain_hbm.1, bf16[512,1024]{1,0:T(8,128)(2,1)} %wq_hbm.1, bf16[8192,256]{1,0:T(8,128)(2,1)} %wkv_hbm.1, bf16[1024,512]{1,0:T(8,128)(2,1)} %wo_hbm.1, ...), custom_call_target="tpu_custom_call" | custom-call | tf_op jit(solution)/shard_map/decode/pallas_call | solution.py:344
  59.1 0.7 %copy.12 = bf16[1,128,512]{2,1,0:T(8,128)(2,1)} copy(bf16[1,128,512]{2,1,0:T(8,128)(2,1)S(1)} %decode.1) | data formatting | bytes 262144

commit v3 on v2

--- a/solution.py
+++ b/solution.py
@@ -58,8 +58,8 @@
     hid_hbm, span_hbm, gain_hbm, wq_hbm, wkv_hbm, wo_hbm, cache_hbm, len_hbm, route_hbm, freq_hbm,
     out_ref,
     hid, span, gain, wq, wkvs, wkv, wo, cache, lens, route, freq,
-    outbox, inbox, proj_out, proj_in, heads_all, part_out, part_in, hid_all, qs, os_,
-    load_sem, box_sem, proj_sem, heads_sem, part_sem, hid_sem,
+    outbox, inbox, proj_out, proj_in, sq, heads_all, part_out, part_in, hid_all, qs, os_,
+    load_sem, box_sem, proj_sem, sq_sem, heads_sem, part_sem, hid_sem,
 ):
     n_role, n_req, n_tp = dims
     role, req, tp = lax.axis_index("role"), lax.axis_index("req"), lax.axis_index("tp")
@@ -79,8 +79,8 @@
 
     steps = [(a, b) for a in range(side) for b in range(side)]
     steps.sort(key=lambda s: -far(s[0], side) - far(s[1], side))
-    req_steps = steps[:-1]
-    pool_steps = [(flip, s) for s in steps for flip in (False, True)]
+    req_steps = steps[:-1] if side != 4 else [(2, 2), (1, 2), (3, 2), (2, 1), (2, 3), (1, 1), (3, 3), (1, 3), (3, 1), (0, 2), (2, 0), (0, 1), (0, 3), (1, 0), (3, 0)]
+    pool_steps = [(flip, s) for flip in (False, True) for s in req_steps + [(0, 0)]]
     pool_steps.remove((False, (0, 0)))
     tp_steps = sorted(range(1, n_tp), key=lambda k: -far(k, n_tp))
 
@@ -118,13 +118,12 @@
             loads[name] = pltpu.make_async_copy(src, dst, load_sem.at[index])
             loads[name].start()
 
-    load(range(4))
     barrier = pltpu.get_barrier_semaphore()
     greeted = [pool_peer(k)[1] for k in pool_steps]
     greeted += [tp_peer(k)[1] for k in tp_steps]
     for device in greeted:
         pl.semaphore_signal(barrier, inc=1, device_id=device, device_id_type=MESH)
-    load(range(4, len(arrays)))
+    load(range(len(arrays)))
 
     def exchange(peers, peer, src, dst, sems):
         for k in peers:
@@ -140,20 +139,18 @@
 
     def project(rows, step, gain_row):
         wide = rows.astype(F32)
-        squares = jnp.sum(wide * wide, axis=1, keepdims=True)
-        squares = jnp.broadcast_to(squares, (reqs, HD)).reshape(n_req, local, HD)
-        main = squares.astype(BF16).astype(F32)
         mixed = (wide * gain_row).astype(BF16)
         both = jnp.concatenate([dot(mixed, wq[...]), dot(mixed, wkvs[...])], axis=1)
         both = both.reshape(n_req, local, -1)
         half = both.shape[2] // 2
-        upper = jnp.concatenate([both[:, :, :half], main], axis=2)
-        lower = jnp.concatenate([both[:, :, half:], squares - main], axis=2)
-        proj_out[step] = jnp.concatenate([upper, lower], axis=1).astype(BF16)
-
-    def send_projection(step):
+        proj_out[step] = jnp.concatenate([both[:, :, :half], both[:, :, half:]], axis=1).astype(BF16)
+
+    def send_projection(rows, step):
         exchange(req_steps, req_peer, lambda other: proj_out.at[step, other],
                  proj_in.at[step, req], proj_sem.at[step])
+        wide = rows.astype(F32)
+        sq[step, pl.ds(req, 1)] = to_row(jnp.sum(wide * wide, axis=1, keepdims=True)).reshape(1, 1, reqs)
+        exchange(req_steps, req_peer, lambda other: sq.at[step, req], sq.at[step, req], sq_sem.at[step])
 
     for name in ("hid", "gain", "wkvs", "wq"):
         loads[name].wait()
@@ -162,7 +159,7 @@
     gain_row = jnp.sum(jnp.where(iota(gains.shape, 0) == req, gains, 0.0), axis=0, keepdims=True)
     project(hid[...], 0, gain_row)
     pl.semaphore_wait(barrier, len(greeted))
-    send_projection(0)
+    send_projection(hid[...], 0)
 
     for name in ("route", "freq", "lens", "span", "wkv"):
         loads[name].wait()
@@ -217,18 +214,19 @@
         item = lax.rem(line, total)
         want = (item // CAP) * chunk + part * CAP + lax.rem(item, CAP)
         sorted_ = dot(jnp.where(iota(sel, 1) == want, 1.0, 0.0).astype(BF16), arrived)
-        key_in = sorted_[0:total].astype(BF16)
-        value_in = sorted_[total:2 * total].astype(BF16)
-        target = (sorted_[2 * total:3 * total] - 1.0) * float(SLOTS) + sorted_[3 * total:]
-        target = jnp.where(sorted_[2 * total:3 * total] > 0.5, target, -1.0)
-        target_row = to_row(target[:, 0:1]).astype(jnp.int32)
-        ones = jnp.ones((total, HD), BF16)
-        for b in range(local):
-            hot = jnp.where(iota((SLOTS, total), 0) + b * SLOTS == target_row, 1.0, 0.0).astype(BF16)
-            hit = dot(hot, ones) > 0.5
-            for lo, rows in ((0, key_in), (HD, value_in)):
-                old = cache[b, 0:SLOTS, lo:lo + HD]
-                cache[b, 0:SLOTS, lo:lo + HD] = jnp.where(hit, dot(hot, rows), old.astype(F32)).astype(BF16)
+        ask, spot = sorted_[2 * total:3 * total], sorted_[3 * total:]
+        target = jnp.where(ask > 0.5, (ask - 1.0) * float(SLOTS) + spot, -1.0)
+        eye = iota((total, total), 0) == iota((total, total), 1)
+        target_row = jnp.sum(jnp.where(eye, target[:, :total], 0.0), axis=0, keepdims=True).astype(jnp.int32)
+        handed = jnp.concatenate(
+            [sorted_[0:total], sorted_[total:2 * total], jnp.ones((total, HD), F32)], axis=1).astype(BF16)
+        hot = jnp.where(iota((local * SLOTS, total), 0) == target_row, 1.0, 0.0).astype(BF16)
+        put = dot(hot, handed).reshape(local, SLOTS, 3 * HD)
+        hit = put[:, :, 2 * HD:] > 0.5
+        old = cache[:, 0:SLOTS, :].astype(F32)
+        cache[:, 0:SLOTS, :] = jnp.concatenate(
+            [jnp.where(hit, put[:, :, 0:HD], old[:, :, 0:HD]),
+             jnp.where(hit, put[:, :, HD:2 * HD], old[:, :, HD:])], axis=2).astype(BF16)
 
     loads["cache"].wait()
     box_wait = arrivals(inbox.at[pl.ds(0, (owners - 1) * chunk)], box_sem)
@@ -241,17 +239,22 @@
         last = step == STEPS - 1
         if step > 0:
             project(hidden[...], step, gain_row)
-            send_projection(step)
+            send_projection(hidden[...], step)
         proj_wait = arrivals(proj_in.at[step, pl.ds(0, n_req - 1)], proj_sem.at[step])
         proj_in[step, pl.ds(req, 1)] = proj_out[step, pl.ds(req, 1)]
+        sq_wait = arrivals(sq.at[step, pl.ds(0, n_req - 1)], sq_sem.at[step])
+        sq_wait.wait_recv()
+        squares = jnp.sum(sq[step].reshape(n_req, reqs), axis=0, keepdims=True)
+        grid = (local, reqs)
+        own = jnp.sum(
+            jnp.where(iota(grid, 1) == iota(grid, 0) + req * local,
+                      jnp.broadcast_to(squares, grid), 0.0), axis=1, keepdims=True)
+        scale = lax.rsqrt(own / (n_req * width) + EPS)
         proj_wait.wait_recv()
         summed = proj_in[step, 0].astype(F32)
         for k in range(1, n_req):
             summed += proj_in[step, k].astype(F32)
-        half = summed.shape[1] - HD
-        own = summed[:local, half:half + 1] + summed[local:, half:half + 1]
-        scale = lax.rsqrt(own / (n_req * width) + EPS)
-        flat = jnp.concatenate([summed[:local, :half], summed[local:, :half]], axis=1) * scale
+        flat = jnp.concatenate([summed[:local], summed[local:]], axis=1) * scale
         cosine, sine = tables[step]
         for h in range(heads):
             qs[pl.ds(h, local, stride=heads), :] = turn(flat[:, h * HD:(h + 1) * HD], cosine, sine)
@@ -322,7 +325,7 @@
         hid_wait = arrivals(target.at[pl.ds(0, (n_tp - 1) * rows_tp)], hid_sem.at[step])
         hid_wait.wait_recv()
         hidden = hid_all
-        sent += [proj_wait, heads_wait, part_wait, hid_wait]
+        sent += [sq_wait, proj_wait, heads_wait, part_wait, hid_wait]
     for item in sent:
         item.wait_send()
 
@@ -360,8 +363,9 @@
             vmem(freq.shape, F32),
             vmem((owners * 4 * CAP, HD), BF16),
             vmem((owners * 4 * CAP, HD), BF16),
-            vmem((STEPS, n_req, 2 * local, cols // 2 + HD), BF16),
-            vmem((STEPS, n_req, 2 * local, cols // 2 + HD), BF16),
+            vmem((STEPS, n_req, 2 * local, cols // 2), BF16),
+            vmem((STEPS, n_req, 2 * local, cols // 2), BF16),
+            vmem((STEPS, n_req, 1, reqs), F32),
             vmem((STEPS, n_req, 2 * local, heads * HD // 2), BF16),
             vmem((STEPS, n_tp, reqs // n_tp, width), BF16),
             vmem((STEPS, n_tp, reqs // n_tp, width), BF16),
@@ -370,6 +374,7 @@
             vmem((local * heads, HD), F32),
             sems((11,)),
             sems((2,)),
+            sems((STEPS, 2)),
             sems((STEPS, 2)),
             sems((STEPS, 2)),
             sems((STEPS, 2)),

time: 60 us -> 58.6 us (0.977)
  Pallas kernels: 59.1 us -> 57.6 us
    pallas_call x1, Pallas kernels: 59.1 us -> 57.6 us  [on_device(): pl.pallas_call(functools.partial(kernel, dims), out_shape=pltpu.VMEM(deco...]
where the time goes in v3:
time: 58.6 us; the launch traced here: 58.2 us
  Pallas kernels  57.6 us (98%)
  local copies, waits for them, and re-layouts  0.66 us (1%)
    pallas_call x1, Pallas kernels, on_device(): pl.pallas_call(functools.partial(kernel, dims), out_shape=pltpu.VMEM(deco...  57.6 us

profile of v3, /device:TPU:24, one launch (start us, length us, event | category | flops | bytes accessed | tf_op | source)
XLA Modules:
  0.0 58.2 jit_solution(14660037846545631812)
XLA Ops:
  0.0 57.6 %decode.1 = bf16[1,128,512]{2,1,0:T(8,128)(2,1)S(1)} custom-call(bf16[1,128,512]{2,1,0:T(8,128)(2,1)} %hid_hbm.1, bf16[1,64,8192]{2,1,0:T(8,128)(2,1)} %span_hbm.1, bf16[8192]{0:T(1024)(128)(2,1)} %gain_hbm.1, bf16[512,1024]{1,0:T(8,128)(2,1)} %wq_hbm.1, bf16[8192,256]{1,0:T(8,128)(2,1)} %wkv_hbm.1, bf16[1024,512]{1,0:T(8,128)(2,1)} %wo_hbm.1, ...), custom_call_target="tpu_custom_call" | custom-call | tf_op jit(solution)/shard_map/decode/pallas_call | solution.py:347
  57.6 0.7 %copy.12 = bf16[1,128,512]{2,1,0:T(8,128)(2,1)} copy(bf16[1,128,512]{2,1,0:T(8,128)(2,1)S(1)} %decode.1) | data formatting | bytes 262144

commit v4 on v3

--- a/solution.py
+++ b/solution.py
@@ -83,6 +83,8 @@
     pool_steps = [(flip, s) for flip in (False, True) for s in req_steps + [(0, 0)]]
     pool_steps.remove((False, (0, 0)))
     tp_steps = sorted(range(1, n_tp), key=lambda k: -far(k, n_tp))
+    if n_tp == 8:
+        tp_steps = [4, 3, 5, 6, 2, 1, 7]
 
     def req_peer(step, flip=False):
         other = lax.rem(req // side + step[0], side) * side + lax.rem(lax.rem(req, side) + step[1], side)
@@ -99,8 +101,8 @@
     first = pl.multiple_of(req * width, width)
     loads = {}
     arrays = [
+        ("gain", gain_hbm, gain),
         ("hid", hid_hbm.at[0], hid),
-        ("gain", gain_hbm, gain),
         ("wkvs", wkv_hbm.at[pl.ds(first, width)], wkvs),
         ("wq", wq_hbm, wq),
         ("route", route_hbm, route),
@@ -140,6 +142,9 @@
     def project(rows, step, gain_row):
         wide = rows.astype(F32)
         mixed = (wide * gain_row).astype(BF16)
+        if step == 0:
+            loads["wkvs"].wait()
+            loads["wq"].wait()
         both = jnp.concatenate([dot(mixed, wq[...]), dot(mixed, wkvs[...])], axis=1)
         both = both.reshape(n_req, local, -1)
         half = both.shape[2] // 2
@@ -152,11 +157,11 @@
         sq[step, pl.ds(req, 1)] = to_row(jnp.sum(wide * wide, axis=1, keepdims=True)).reshape(1, 1, reqs)
         exchange(req_steps, req_peer, lambda other: sq.at[step, req], sq.at[step, req], sq_sem.at[step])
 
-    for name in ("hid", "gain", "wkvs", "wq"):
-        loads[name].wait()
+    loads["gain"].wait()
     gains = jnp.concatenate(
         [gain[j * width:(j + 1) * width].astype(F32).reshape(1, width) for j in range(n_req)], axis=0)
     gain_row = jnp.sum(jnp.where(iota(gains.shape, 0) == req, gains, 0.0), axis=0, keepdims=True)
+    loads["hid"].wait()
     project(hid[...], 0, gain_row)
     pl.semaphore_wait(barrier, len(greeted))
     send_projection(hid[...], 0)
@@ -271,28 +276,51 @@
             return jnp.concatenate(
                 [dot_t(queries[b], cache[b, lo:hi, 0:HD]) for b in range(local)], axis=0) * inverse
 
-        late = scores(SLOTS, ctx)
-        live = iota(late.shape, 1) + SLOTS < len_rows
-        late = jnp.where(live, late, FLOOR)
+        def mix(weights, lo, hi):
+            return jnp.concatenate([
+                dot(weights[b * heads:(b + 1) * heads].astype(BF16), cache[b, lo:hi, HD:])
+                for b in range(local)
+            ], axis=0)
+
         if step == 0:
+            late = scores(SLOTS, ctx)
+            live = iota(late.shape, 1) + SLOTS < len_rows
+            late = jnp.where(live, late, FLOOR)
+            wide = qs[...].astype(BF16).astype(F32)
+            news = [jnp.sum(wide * k, axis=1, keepdims=True) * inverse for k, _ in fresh]
+            first_top = jnp.max(late, axis=1, keepdims=True)
+            for new in news:
+                first_top = jnp.maximum(first_top, new)
+            late = jnp.exp(late - first_top)
+            norm = jnp.sum(late, axis=1, keepdims=True)
+            mixture = mix(late, SLOTS, ctx)
+            for new, (_, v) in zip(news, fresh):
+                new = jnp.exp(new - first_top)
+                norm += new
+                mixture += new.astype(BF16).astype(F32) * v
             box_wait.wait_recv()
             place_handed()
-        early = scores(0, SLOTS)
-        wide = qs[...].astype(BF16).astype(F32)
-        news = [jnp.sum(wide * k, axis=1, keepdims=True) * inverse for k, _ in fresh]
-        top = jnp.maximum(jnp.max(late, axis=1, keepdims=True), jnp.max(early, axis=1, keepdims=True))
-        for new in news:
-            top = jnp.maximum(top, new)
-        early, late = jnp.exp(early - top), jnp.exp(late - top)
-        norm = jnp.sum(early, axis=1, keepdims=True) + jnp.sum(late, axis=1, keepdims=True)
-        weights = jnp.concatenate([early, late], axis=1)
-        mixture = jnp.concatenate([
-            dot(weights[b * heads:(b + 1) * heads].astype(BF16), cache[b, :, HD:]) for b in range(local)
-        ], axis=0)
-        for new, (_, v) in zip(news, fresh):
-            new = jnp.exp(new - top)
-            norm += new
-            mixture += new.astype(BF16).astype(F32) * v
+            early = scores(0, SLOTS)
+            top = jnp.maximum(first_top, jnp.max(early, axis=1, keepdims=True))
+            early = jnp.exp(early - top)
+            shrink = jnp.exp(first_top - top)
+            norm = norm * shrink + jnp.sum(early, axis=1, keepdims=True)
+            mixture = mixture * shrink + mix(early, 0, SLOTS)
+        else:
+            full = scores(0, ctx)
+            full = jnp.where(iota(full.shape, 1) < len_rows, full, FLOOR)
+            wide = qs[...].astype(BF16).astype(F32)
+            news = [jnp.sum(wide * k, axis=1, keepdims=True) * inverse for k, _ in fresh]
+            top = jnp.max(full, axis=1, keepdims=True)
+            for new in news:
+                top = jnp.maximum(top, new)
+            full = jnp.exp(full - top)
+            norm = jnp.sum(full, axis=1, keepdims=True)
+            mixture = mix(full, 0, ctx)
+            for new, (_, v) in zip(news, fresh):
+                new = jnp.exp(new - top)
+                norm += new
+                mixture += new.astype(BF16).astype(F32) * v
         os_[...] = mixture / norm
         pieces = [os_[pl.ds(h, local, stride=heads), :] for h in range(heads)]
         mid = heads // 2

time: 58.6 us -> 58.4 us (level)
  no operation moved by 1% of the time
where the time goes in v4:
time: 58.4 us; the launch traced here: 58.2 us
  Pallas kernels  57.5 us (98%)
  local copies, waits for them, and re-layouts  0.66 us (1%)
    pallas_call x1, Pallas kernels, on_device(): pl.pallas_call(functools.partial(kernel, dims), out_shape=pltpu.VMEM(deco...  57.5 us

profile of v4, /device:TPU:24, one launch (start us, length us, event | category | flops | bytes accessed | tf_op | source)
XLA Modules:
  0.0 58.2 jit_solution(9358318674722067378)
XLA Ops:
  0.0 57.5 %decode.1 = bf16[1,128,512]{2,1,0:T(8,128)(2,1)S(1)} custom-call(bf16[1,128,512]{2,1,0:T(8,128)(2,1)} %hid_hbm.1, bf16[1,64,8192]{2,1,0:T(8,128)(2,1)} %span_hbm.1, bf16[8192]{0:T(1024)(128)(2,1)} %gain_hbm.1, bf16[512,1024]{1,0:T(8,128)(2,1)} %wq_hbm.1, bf16[8192,256]{1,0:T(8,128)(2,1)} %wkv_hbm.1, bf16[1024,512]{1,0:T(8,128)(2,1)} %wo_hbm.1, ...), custom_call_target="tpu_custom_call" | custom-call | tf_op jit(solution)/shard_map/decode/pallas_call | solution.py:375
  57.5 0.7 %copy.12 = bf16[1,128,512]{2,1,0:T(8,128)(2,1)} copy(bf16[1,128,512]{2,1,0:T(8,128)(2,1)S(1)} %decode.1) | data formatting | bytes 262144
